TPU v7x, 32 devices: a whole 2x2x4 slice. The times are simulated.
32 devices in a mesh: groups: 2 (over x), space: 16 (over z, y, core).
Axes of the slice: x: 2, y: 2, z: 4, core: 2. Of those that a mesh axis runs over, the one named last changes fastest.
Arguments:
- snapshots: bfloat16 [256, 128, 128], P(('groups', 'space')), parts along dimension 0, may hold values from -6 to 6
- weights: bfloat16 [256, 128, 1024], P(('groups', 'space')), parts along dimension 0, may hold values from -6 to 6
- neighbours: int32 [256, 8], P(('groups', 'space')), parts along dimension 0, may hold values from 0 to 127, as said below
- time_of: int32 [256], P('groups'), parts along dimension 0, may hold values from 0 to 127, each once
Outputs:
- new_weights: float32 [256, 128, 1024], P(('groups', 'space')), parts along dimension 0
- cell_error: float32 [256, 128], P(('groups', 'space')), parts along dimension 0
There are 2 independent parts, one for each index of `groups`. A program takes and returns all parts, laid end to end along the dimension named above; each array names one. Nothing has to cross between parts.
Inputs may be any that keep to these rules, and one draw needn't show every extreme that they name: `neighbours`: row g lists 8 groups in a drawn order: g itself, g - 4, g + 4, and 5 more within 4 groups of g, all counted cyclically modulo 128; entries may repeat. `time_of`: each time index appears once.
All inputs are finite; a program needn't handle non-finite values.
Results may differ from a plain program's by a relative error of at most 0.002.
Values may be sent and summed in bfloat16 or wider, within the bound.
A program may use at most 64 MiB of HBM per device.

v0:
```python
import jax
import jax.numpy as jnp
from jax import lax
from jax.sharding import PartitionSpec as P

HALO = 4


def extended(x, sides, width):
    for axis, dim in sides:
        size, length = (lax.axis_size(axis), x.shape[dim])
        up = [(i, (i + 1) % size) for i in range(size)]
        down = [(j, i) for i, j in up]
        last = lax.slice_in_dim(x, length - width, length, axis=dim)
        initial = lax.slice_in_dim(x, 0, width, axis=dim)
        before = lax.ppermute(last, axis, up)
        after = lax.ppermute(initial, axis, down)
        x = jnp.concatenate([before, x, after], axis=dim)
    return x


def shards(snapshots, weights, neighbours, time_of):
    step_rate = 100.0
    g_dev = weights.shape[0]
    width = weights.shape[1]
    span = weights.shape[2]
    n_dev = lax.axis_size("space")
    total = time_of.shape[0]
    owned = lax.all_to_all(snapshots, "space", split_axis=1, concat_axis=0, tiled=True)
    padded = extended(owned, (("space", 1),), HALO)
    order = jnp.argsort(time_of)
    ordered = padded[order]
    target = jnp.roll(ordered[:, HALO : HALO + g_dev], -1, 0)
    first = lax.axis_index("space") * g_dev
    all_groups = g_dev * n_dev
    here = jnp.arange(g_dev, dtype=jnp.int32)
    local = (neighbours - (first + here)[:, None] + HALO) % all_groups + here[:, None]
    scale = 1.0 / jnp.sqrt(jnp.float32(span))
    rows_step = min(total, 256)
    turns = total // rows_step

    def block_rows(turn):
        rows = lax.dynamic_slice_in_dim(ordered, turn * rows_step, rows_step, 0)
        goal = lax.dynamic_slice_in_dim(target, turn * rows_step, rows_step, 0).astype(jnp.float32)
        inputs = rows[:, local].reshape(rows_step, g_dev, span)
        live = (turn * rows_step + jnp.arange(rows_step) < total - 1).astype(jnp.float32)[
            :, None, None
        ]
        return (inputs, goal, live)

    def add_grad(turn, grad):
        inputs, goal, live = block_rows(turn)
        pred = (
            jnp.einsum("tgc,goc->tgo", inputs, weights, preferred_element_type=jnp.float32) * scale
        )
        resid = ((pred - goal) * live).astype(jnp.bfloat16)
        return grad + jnp.einsum("tgo,tgc->goc", resid, inputs, preferred_element_type=jnp.float32)

    grad = lax.fori_loop(0, turns, add_grad, jnp.zeros((g_dev, width, span), jnp.float32))
    new_weights = weights.astype(jnp.float32) - step_rate * (grad * (2.0 * scale / (total - 1)))
    new_rounded = new_weights.astype(jnp.bfloat16)

    def add_error(turn, error):
        inputs, goal, live = block_rows(turn)
        after = (
            jnp.einsum("tgc,goc->tgo", inputs, new_rounded, preferred_element_type=jnp.float32)
            * scale
            - goal
        ) * live
        return error + jnp.sum(after * after, axis=0)

    error = lax.fori_loop(0, turns, add_error, jnp.zeros((g_dev, width), jnp.float32))
    return (new_weights, error / (total - 1))


def solution(mesh):
    return jax.shard_map(
        shards,
        mesh=mesh,
        in_specs=(
            P(("groups", "space"), None, None),
            P(("groups", "space"), None, None),
            P(("groups", "space"), None),
            P("groups"),
        ),
        out_specs=(P(("groups", "space"), None, None), P(("groups", "space"), None)),
        check_vma=False,
    )
```

profile of v0, /device:TPU:0, one launch (start us, length us, event | category | flops | bytes accessed | tf_op | source)
XLA Modules:
  0.0 38.4 jit_solution(6387515284216943299)
XLA Ops:
  0.6 1.8 %copy.21 = bf16[8,128,128]{2,0,1:T(8,128)(2,1)} copy(bf16[8,128,128]{2,1,0:T(8,128)(2,1)} %param.4) | data formatting | bytes 524288 | tf_op args[0]
  2.5 7.4 %all-to-all-start = ((bf16[8,128,128]{2,0,1:T(8,128)(2,1)}), bf16[8,128,128]{2,0,1:T(8,128)(2,1)S(1)}, u32[]{:S(2)}, u32[]{:S(2)}) async-start(bf16[8,128,128]{2,0,1:T(8,128)(2,1)} %copy.21), calls=%async_computation | async-start | bytes 524288 | tf_op jit(solution)/shard_map/all_to_all | solution.py:29
  9.9 3.2 %sort.17 = (s32[128]{0:T(128)}, s32[128]{0:T(128)S(1)}) sort(s32[128]{0:T(128)} %param.7, s32[128]{0:T(128)S(1)} %iota.22), dimensions={0}, to_apply=%region_0.0 | sort | flops 896 | bytes 2048 | tf_op jit(solution)/shard_map/jit(argsort)/sort | solution.py:31
  13.1 0.8 %compare_select_fusion = s32[8,8]{1,0:T(8,128)S(1)} fusion(s32[8,8]{1,0:T(8,128)} %param.6, s32[8]{0:T(128)S(1)} %iota_add_fusion), kind=kLoop, calls=%fused_computation.28 | loop fusion | flops 1088 | bytes 544 | tf_op jit(solution)/shard_map/while/body/eval_jaxpr/select_n | solution.py:45
  13.8 6.1 %all-to-all-done = bf16[8,128,128]{2,0,1:T(8,128)(2,1)S(1)} async-done(((bf16[8,128,128]{2,0,1:T(8,128)(2,1)}), bf16[8,128,128]{2,0,1:T(8,128)(2,1)S(1)}, u32[]{:S(2)}, u32[]{:S(2)}) %all-to-all-start) | async-done | bytes 262176 | tf_op jit(solution)/shard_map/all_to_all | solution.py:29
  19.9 0.1 fusion.63
  20.0 0.1 collective-permute-start
  20.1 4.4 %collective-permute-start.1 = (bf16[128,4,128]{2,1,0:T(4,128)(2,1)S(1)}, bf16[128,4,128]{2,1,0:T(4,128)(2,1)S(1)}, u32[]{:S(2)}, u32[]{:S(2)}) collective-permute-start(bf16[128,4,128]{2,1,0:T(4,128)(2,1)S(1)} %get-tuple-element.33), channel_id=1, source_target_pairs={{1,0},{2,1},{3,2},{4,3},{5,4},{6,5},{7,6},{8,7},{9,8},{10,9},{11,1... | collective-permute-start | bytes 393224 | tf_op jit(solution)/shard_map/ppermute | solution.py:17
  24.5 0.1 reshape.30
  24.6 2.6 %collective-permute-done = bf16[128,4,128]{2,1,0:T(4,128)(2,1)S(1)} collective-permute-done((bf16[128,4,128]{2,1,0:T(4,128)(2,1)S(1)}, bf16[128,4,128]{2,1,0:T(4,128)(2,1)S(1)}, u32[]{:S(2)}, u32[]{:S(2)}) %collective-permute-start) | collective-permute-done | bytes 131104 | tf_op jit(solution)/shard_map/ppermute | solution.py:16
  27.2 0.0 collective-permute-done.1
  27.2 0.3 pad_maximum_fusion
  27.5 0.7 %gather_fusion = bf16[128,16,128]{2,1,0:T(8,128)(2,1)S(1)} fusion(bf16[128,16,128]{2,1,0:T(8,128)(2,1)S(1)} %pad_maximum_fusion, s32[1024]{0:T(1024)S(1)} %pad_clamp_fusion.1), kind=kCustom, calls=%fused_computation | custom fusion | bytes 1049088 | tf_op jit(solution)/shard_map/gather | solution.py:32
  28.2 0.1 copy.24
  28.4 0.1 slice.27
  28.4 1.0 %gather_fusion.1 = bf16[64,128,128]{2,1,0:T(8,128)(2,1)S(1)} fusion(bf16[128,16,128]{2,0,1:T(8,128)(2,1)S(1)} %copy.24, s32[1024]{0:T(1024)S(1)} %pad_clamp_fusion), kind=kCustom, calls=%fused_computation.1 | custom fusion | bytes 4194560 | tf_op jit(solution)/shard_map/while/body/eval_jaxpr/gather | solution.py:45
  29.4 5.5 %multiply_subtract_fusion = f32[8,128,1024]{2,1,0:T(8,128)} fusion(bf16[8,128,1024]{2,1,0:T(8,128)(2,1)} %param.5, bf16[8,8,16,8,128]{4,3,2,1,0:T(8,128)(2,1)S(1)} %bitcast.60, f32[128]{0:T(128)S(1)} %compare_convert_fusion, bf16[1,8,128]{2,0,1:T(2,128)(2,1)S(1)} %slice.28, bf16[127,8,128]{2,0,1:T(8,128)(2,1)S(1)} %slice.27), kind=kOutput, calls=%fused_computation.2 | convolution fusion | flops 541065216 | bytes 8651264 | tf_op jit(solution)/shard_map/while/body/eval_jaxpr/tgo,tgc->goc/dot_general | solution.py:57
  34.9 2.9 %fusion.51 = f32[8,128]{1,0:T(8,128)S(1)} fusion(bf16[8,8,16,8,128]{4,3,2,1,0:T(8,128)(2,1)S(1)} %bitcast.61, f32[8,128,1024]{2,1,0:T(8,128)} %multiply_subtract_fusion, f32[128]{0:T(128)S(1)} %compare_convert_fusion, bf16[1,8,128]{2,0,1:T(2,128)(2,1)S(1)} %slice.28, bf16[127,8,128]{2,0,1:T(8,128)(2,1)S(1)} %slice.27), kind=kOutput, calls=%fused_computation.22 | convolution fusion | flops 270662656 | bytes 6558208 | tf_op jit(solution)/shard_map/while/body/eval_jaxpr/tgc,goc->tgo/dot_general | solution.py:66
  37.8 0.6 %broadcast_multiply_fusion = f32[8,128]{1,0:T(8,128)} fusion(f32[8,128]{1,0:T(8,128)S(1)} %fusion.51), kind=kLoop, calls=%fused_computation.37 | loop fusion | flops 1024 | bytes 8192 | tf_op jit(solution)/shard_map/div | solution.py:73
  (8 shorter events, 0.1 us)
Async XLA Ops:
  2.5 17.4 %all-to-all-start = ((bf16[8,128,128]{2,0,1:T(8,128)(2,1)}), bf16[8,128,128]{2,0,1:T(8,128)(2,1)S(1)}, u32[]{:S(2)}, u32[]{:S(2)}) async-start(bf16[8,128,128]{2,0,1:T(8,128)(2,1)} %copy.21), calls=%async_computation | async-start | bytes 524288 | tf_op jit(solution)/shard_map/all_to_all | solution.py:29
  20.0 7.1 %collective-permute-start = (bf16[128,4,128]{2,1,0:T(4,128)(2,1)S(1)}, bf16[128,4,128]{2,1,0:T(4,128)(2,1)S(1)}, u32[]{:S(2)}, u32[]{:S(2)}) collective-permute-start(bf16[128,4,128]{2,1,0:T(4,128)(2,1)S(1)} %get-tuple-element.32), channel_id=1, source_target_pairs={{0,1},{1,2},{2,3},{3,4},{4,5},{5,6},{6,7},{7,8},{8,9},{9,10},{10,1... | collective-permute-start | bytes 393224 | tf_op jit(solution)/shard_map/ppermute | solution.py:16
  20.1 7.1 %collective-permute-start.1 = (bf16[128,4,128]{2,1,0:T(4,128)(2,1)S(1)}, bf16[128,4,128]{2,1,0:T(4,128)(2,1)S(1)}, u32[]{:S(2)}, u32[]{:S(2)}) collective-permute-start(bf16[128,4,128]{2,1,0:T(4,128)(2,1)S(1)} %get-tuple-element.33), channel_id=1, source_target_pairs={{1,0},{2,1},{3,2},{4,3},{5,4},{6,5},{7,6},{8,7},{9,8},{10,9},{11,1... | collective-permute-start | bytes 393224 | tf_op jit(solution)/shard_map/ppermute | solution.py:17
where the time goes:
time: 38.7 us; the launch traced here: 38.4 us
  starting transfers between devices  11.9 us (31%)
  waiting for transfers between devices  8.62 us (22%)
  matrix products  8.4 us (22%)
  other arithmetic  4.87 us (13%)
  local copies, waits for them, and re-layouts  3.91 us (10%)
  between operations  0.72 us (2%)
    all_to_all x1, starting transfers between devices, shards(): lax.all_to_all(snapshots, 'space', split_axis=1, concat_axis=0, tiled=True)  7.39 us
    all_to_all x1, waiting for transfers between devices, shards(): lax.all_to_all(snapshots, 'space', split_axis=1, concat_axis=0, tiled=True)  6.06 us
    dot_general x1, matrix products, add_grad(): jnp.einsum('tgo,tgc->goc', resid, inputs, preferred_element_type=jnp.floa...  5.49 us
    ppermute x1, starting transfers between devices, extended(): after = lax.ppermute(initial, axis, down)  4.43 us
    sort x1, other arithmetic, shards(): order = jnp.argsort(time_of)  3.19 us
    dot_general x1, matrix products, add_error(): jnp.einsum('tgc,goc->tgo', inputs, new_rounded, preferred_element_type=jn...  2.91 us
    ppermute x1, waiting for transfers between devices, extended(): before = lax.ppermute(last, axis, up)  2.55 us
    unnamed x1, local copies, waits for them, and re-layouts  1.83 us
  transfers between devices with their start and end apart: 3, of which 2 were waited for; matrix products, arithmetic and copies ran while one was open for 11% of the time, Pallas kernels for 0%

commit v1 on v0

--- a/solution.py
+++ b/solution.py
@@ -4,6 +4,13 @@
 from jax.sharding import PartitionSpec as P
 
 HALO = 4
+
+
+def exchange_blocks(x, axis, split, join):
+    devices = lax.axis_size(axis)
+    blocks = jnp.stack(jnp.split(x, devices, axis=split), axis=0)
+    blocks = lax.all_to_all(blocks, axis, split_axis=0, concat_axis=0)
+    return jnp.concatenate(blocks, axis=join)
 
 
 def extended(x, sides, width):
@@ -26,7 +33,7 @@
     span = weights.shape[2]
     n_dev = lax.axis_size("space")
     total = time_of.shape[0]
-    owned = lax.all_to_all(snapshots, "space", split_axis=1, concat_axis=0, tiled=True)
+    owned = exchange_blocks(snapshots, "space", 1, 0)
     padded = extended(owned, (("space", 1),), HALO)
     order = jnp.argsort(time_of)
     ordered = padded[order]

time: 38.7 us -> 58.8 us (1.52); the launches traced: 38.4 us -> 57.7 us
  local copies, waits for them, and re-layouts: 3.91 us -> 23.2 us
    unnamed x1 -> x15, local copies, waits for them, and re-layouts: 1.83 us -> 19.9 us
    another operation x0 -> x1, local copies, waits for them, and re-layouts: none -> 1.32 us  [exchange_blocks(): blocks = jnp.stack(jnp.split(x, devices, axis=split), axis=0)]
  transfers between devices with their start and end apart: 3 -> 3, of which waited for: 2 -> 2; matrix products, arithmetic and copies ran while one was open for 11% -> 7% of each run, Pallas kernels for 0% -> 0%
where the time goes in v1:
time: 58.8 us; the launch traced here: 57.7 us
  local copies, waits for them, and re-layouts  23.2 us (39%)
  starting transfers between devices  11.9 us (20%)
  waiting for transfers between devices  8.62 us (15%)
  matrix products  8.4 us (14%)
  other arithmetic  4.87 us (8%)
  between operations  0.72 us (1%)
    unnamed x15, local copies, waits for them, and re-layouts  19.9 us
    all_to_all x1, starting transfers between devices, exchange_blocks(): blocks = lax.all_to_all(blocks, axis, split_axis=0, concat_axis=0)  7.39 us
    all_to_all x1, waiting for transfers between devices, exchange_blocks(): blocks = lax.all_to_all(blocks, axis, split_axis=0, concat_axis=0)  6.06 us
    dot_general x1, matrix products, add_grad(): jnp.einsum('tgo,tgc->goc', resid, inputs, preferred_element_type=jnp.floa...  5.49 us
    ppermute x1, starting transfers between devices, extended(): after = lax.ppermute(initial, axis, down)  4.43 us
    sort x1, other arithmetic, shards(): order = jnp.argsort(time_of)  3.19 us
    dot_general x1, matrix products, add_error(): jnp.einsum('tgc,goc->tgo', inputs, new_rounded, preferred_element_type=jn...  2.91 us
    ppermute x1, waiting for transfers between devices, extended(): before = lax.ppermute(last, axis, up)  2.55 us
  transfers between devices with their start and end apart: 3, of which 2 were waited for; matrix products, arithmetic and copies ran while one was open for 7% of the time, Pallas kernels for 0%

profile of v1, /device:TPU:0, one launch (start us, length us, event | category | flops | bytes accessed | tf_op | source)
XLA Modules:
  0.0 57.7 jit_solution(5357058615090368308)
XLA Ops:
  0.6 1.3 %constant_dynamic-update-slice_fusion.15 = bf16[16,8,8,128]{3,2,1,0:T(8,128)(2,1)} fusion(bf16[8,128,128]{2,1,0:T(8,128)(2,1)} %param.4), kind=kLoop, calls=%fused_computation.43 | loop fusion | bytes 32768
  2.0 1.3 %constant_dynamic-update-slice_fusion.14 = bf16[16,8,8,128]{3,2,1,0:T(8,128)(2,1)} fusion(bf16[16,8,8,128]{3,2,1,0:T(8,128)(2,1)} %constant_dynamic-update-slice_fusion.15, bf16[8,128,128]{2,1,0:T(8,128)(2,1)} %param.4), kind=kLoop, calls=%fused_computation.42 | loop fusion | bytes 32768
  3.3 1.3 %constant_dynamic-update-slice_fusion.13 = bf16[16,8,8,128]{3,2,1,0:T(8,128)(2,1)} fusion(bf16[16,8,8,128]{3,2,1,0:T(8,128)(2,1)} %constant_dynamic-update-slice_fusion.14, bf16[8,128,128]{2,1,0:T(8,128)(2,1)} %param.4), kind=kLoop, calls=%fused_computation.41 | loop fusion | bytes 32768
  4.6 1.3 %constant_dynamic-update-slice_fusion.12 = bf16[16,8,8,128]{3,2,1,0:T(8,128)(2,1)} fusion(bf16[16,8,8,128]{3,2,1,0:T(8,128)(2,1)} %constant_dynamic-update-slice_fusion.13, bf16[8,128,128]{2,1,0:T(8,128)(2,1)} %param.4), kind=kLoop, calls=%fused_computation.40 | loop fusion | bytes 32768
  5.9 1.3 %constant_dynamic-update-slice_fusion.11 = bf16[16,8,8,128]{3,2,1,0:T(8,128)(2,1)} fusion(bf16[16,8,8,128]{3,2,1,0:T(8,128)(2,1)} %constant_dynamic-update-slice_fusion.12, bf16[8,128,128]{2,1,0:T(8,128)(2,1)} %param.4), kind=kLoop, calls=%fused_computation.39 | loop fusion | bytes 32768
  7.2 1.3 %constant_dynamic-update-slice_fusion.10 = bf16[16,8,8,128]{3,2,1,0:T(8,128)(2,1)} fusion(bf16[16,8,8,128]{3,2,1,0:T(8,128)(2,1)} %constant_dynamic-update-slice_fusion.11, bf16[8,128,128]{2,1,0:T(8,128)(2,1)} %param.4), kind=kLoop, calls=%fused_computation.38 | loop fusion | bytes 32768
  8.6 1.3 %constant_dynamic-update-slice_fusion.9 = bf16[16,8,8,128]{3,2,1,0:T(8,128)(2,1)} fusion(bf16[16,8,8,128]{3,2,1,0:T(8,128)(2,1)} %constant_dynamic-update-slice_fusion.10, bf16[8,128,128]{2,1,0:T(8,128)(2,1)} %param.4), kind=kLoop, calls=%fused_computation.37 | loop fusion | bytes 32768
  9.9 1.3 %constant_dynamic-update-slice_fusion.8 = bf16[16,8,8,128]{3,2,1,0:T(8,128)(2,1)} fusion(bf16[16,8,8,128]{3,2,1,0:T(8,128)(2,1)} %constant_dynamic-update-slice_fusion.9, bf16[8,128,128]{2,1,0:T(8,128)(2,1)} %param.4), kind=kLoop, calls=%fused_computation.36 | loop fusion | bytes 32768
  11.2 1.3 %constant_dynamic-update-slice_fusion.7 = bf16[16,8,8,128]{3,2,1,0:T(8,128)(2,1)} fusion(bf16[16,8,8,128]{3,2,1,0:T(8,128)(2,1)} %constant_dynamic-update-slice_fusion.8, bf16[8,128,128]{2,1,0:T(8,128)(2,1)} %param.4), kind=kLoop, calls=%fused_computation.35 | loop fusion | bytes 32768
  12.5 1.3 %constant_dynamic-update-slice_fusion.6 = bf16[16,8,8,128]{3,2,1,0:T(8,128)(2,1)} fusion(bf16[16,8,8,128]{3,2,1,0:T(8,128)(2,1)} %constant_dynamic-update-slice_fusion.7, bf16[8,128,128]{2,1,0:T(8,128)(2,1)} %param.4), kind=kLoop, calls=%fused_computation.34 | loop fusion | bytes 32768
  13.9 1.3 %constant_dynamic-update-slice_fusion.5 = bf16[16,8,8,128]{3,2,1,0:T(8,128)(2,1)} fusion(bf16[16,8,8,128]{3,2,1,0:T(8,128)(2,1)} %constant_dynamic-update-slice_fusion.6, bf16[8,128,128]{2,1,0:T(8,128)(2,1)} %param.4), kind=kLoop, calls=%fused_computation.33 | loop fusion | bytes 32768
  15.2 1.3 %constant_dynamic-update-slice_fusion.4 = bf16[16,8,8,128]{3,2,1,0:T(8,128)(2,1)} fusion(bf16[16,8,8,128]{3,2,1,0:T(8,128)(2,1)} %constant_dynamic-update-slice_fusion.5, bf16[8,128,128]{2,1,0:T(8,128)(2,1)} %param.4), kind=kLoop, calls=%fused_computation.32 | loop fusion | bytes 32768
  16.5 1.3 %constant_dynamic-update-slice_fusion.3 = bf16[16,8,8,128]{3,2,1,0:T(8,128)(2,1)} fusion(bf16[16,8,8,128]{3,2,1,0:T(8,128)(2,1)} %constant_dynamic-update-slice_fusion.4, bf16[8,128,128]{2,1,0:T(8,128)(2,1)} %param.4), kind=kLoop, calls=%fused_computation.31 | loop fusion | bytes 32768
  17.8 1.3 %constant_dynamic-update-slice_fusion.2 = bf16[16,8,8,128]{3,2,1,0:T(8,128)(2,1)} fusion(bf16[16,8,8,128]{3,2,1,0:T(8,128)(2,1)} %constant_dynamic-update-slice_fusion.3, bf16[8,128,128]{2,1,0:T(8,128)(2,1)} %param.4), kind=kLoop, calls=%fused_computation.30 | loop fusion | bytes 32768
  19.2 1.3 %constant_dynamic-update-slice_fusion.1 = bf16[16,8,8,128]{3,2,1,0:T(8,128)(2,1)} fusion(bf16[16,8,8,128]{3,2,1,0:T(8,128)(2,1)} %constant_dynamic-update-slice_fusion.2, bf16[8,128,128]{2,1,0:T(8,128)(2,1)} %param.4), kind=kLoop, calls=%fused_computation.29 | loop fusion | bytes 32768
  20.5 1.3 %constant_dynamic-update-slice_fusion = bf16[16,8,8,128]{3,2,1,0:T(8,128)(2,1)} fusion(bf16[16,8,8,128]{3,2,1,0:T(8,128)(2,1)} %constant_dynamic-update-slice_fusion.1, bf16[8,128,128]{2,1,0:T(8,128)(2,1)} %param.4), kind=kLoop, calls=%fused_computation.28 | loop fusion | bytes 32768 | tf_op jit(solution)/shard_map/stack | solution.py:11
  21.8 7.4 %all-to-all-start = ((bf16[16,8,8,128]{3,2,1,0:T(8,128)(2,1)}), bf16[16,8,8,128]{3,2,1,0:T(8,128)(2,1)S(1)}, u32[]{:S(2)}, u32[]{:S(2)}) async-start(bf16[16,8,8,128]{3,2,1,0:T(8,128)(2,1)} %constant_dynamic-update-slice_fusion), calls=%async_computation | async-start | bytes 524288 | tf_op jit(solution)/shard_map/all_to_all | solution.py:12
  29.2 3.2 %sort.17 = (s32[128]{0:T(128)}, s32[128]{0:T(128)S(1)}) sort(s32[128]{0:T(128)} %param.7, s32[128]{0:T(128)S(1)} %iota.22), dimensions={0}, to_apply=%region_0.0 | sort | flops 896 | bytes 2048 | tf_op jit(solution)/shard_map/jit(argsort)/sort | solution.py:38
  33.2 6.1 %all-to-all-done = bf16[16,8,8,128]{3,2,1,0:T(8,128)(2,1)S(1)} async-done(((bf16[16,8,8,128]{3,2,1,0:T(8,128)(2,1)}), bf16[16,8,8,128]{3,2,1,0:T(8,128)(2,1)S(1)}, u32[]{:S(2)}, u32[]{:S(2)}) %all-to-all-start) | async-done | bytes 262176 | tf_op jit(solution)/shard_map/all_to_all | solution.py:12
  39.4 4.4 %collective-permute-start.1 = (bf16[128,4,128]{2,1,0:T(4,128)(2,1)S(1)}, bf16[128,4,128]{2,1,0:T(4,128)(2,1)S(1)}, u32[]{:S(2)}, u32[]{:S(2)}) collective-permute-start(bf16[128,4,128]{2,1,0:T(4,128)(2,1)S(1)} %get-tuple-element.33), channel_id=1, source_target_pairs={{1,0},{2,1},{3,2},{4,3},{5,4},{6,5},{7,6},{8,7},{9,8},{10,9},{11,1... | collective-permute-start | bytes 393224 | tf_op jit(solution)/shard_map/ppermute | solution.py:24
  43.9 2.6 %collective-permute-done = bf16[128,4,128]{2,1,0:T(4,128)(2,1)S(1)} collective-permute-done((bf16[128,4,128]{2,1,0:T(4,128)(2,1)S(1)}, bf16[128,4,128]{2,1,0:T(4,128)(2,1)S(1)}, u32[]{:S(2)}, u32[]{:S(2)}) %collective-permute-start) | collective-permute-done | bytes 131104 | tf_op jit(solution)/shard_map/ppermute | solution.py:23
  47.7 1.0 %gather_fusion.1 = bf16[64,128,128]{2,1,0:T(8,128)(2,1)S(1)} fusion(bf16[128,16,128]{2,0,1:T(8,128)(2,1)S(1)} %copy.14, s32[1024]{0:T(1024)S(1)} %pad_clamp_fusion), kind=kCustom, calls=%fused_computation.1 | custom fusion | bytes 4194560 | tf_op jit(solution)/shard_map/while/body/eval_jaxpr/gather | solution.py:52
  48.7 5.5 %multiply_subtract_fusion = f32[8,128,1024]{2,1,0:T(8,128)} fusion(bf16[8,128,1024]{2,1,0:T(8,128)(2,1)} %param.5, bf16[8,8,16,8,128]{4,3,2,1,0:T(8,128)(2,1)S(1)} %bitcast.89, f32[128]{0:T(128)S(1)} %compare_convert_fusion, bf16[1,8,128]{2,0,1:T(2,128)(2,1)S(1)} %slice.28, bf16[127,8,128]{2,0,1:T(8,128)(2,1)S(1)} %slice.27), kind=kOutput, calls=%fused_computation.2 | convolution fusion | flops 541065216 | bytes 8651264 | tf_op jit(solution)/shard_map/while/body/eval_jaxpr/tgo,tgc->goc/dot_general | solution.py:64
  54.2 2.9 %fusion.51 = f32[8,128]{1,0:T(8,128)S(1)} fusion(bf16[8,8,16,8,128]{4,3,2,1,0:T(8,128)(2,1)S(1)} %bitcast.90, f32[8,128,1024]{2,1,0:T(8,128)} %multiply_subtract_fusion, f32[128]{0:T(128)S(1)} %compare_convert_fusion, bf16[1,8,128]{2,0,1:T(2,128)(2,1)S(1)} %slice.28, bf16[127,8,128]{2,0,1:T(8,128)(2,1)S(1)} %slice.27), kind=kOutput, calls=%fused_computation.22 | convolution fusion | flops 270662656 | bytes 6558208 | tf_op jit(solution)/shard_map/while/body/eval_jaxpr/tgc,goc->tgo/dot_general | solution.py:73
  (17 shorter events, 2.8 us)
Async XLA Ops:
  21.8 17.4 %all-to-all-start = ((bf16[16,8,8,128]{3,2,1,0:T(8,128)(2,1)}), bf16[16,8,8,128]{3,2,1,0:T(8,128)(2,1)S(1)}, u32[]{:S(2)}, u32[]{:S(2)}) async-start(bf16[16,8,8,128]{3,2,1,0:T(8,128)(2,1)} %constant_dynamic-update-slice_fusion), calls=%async_computation | async-start | bytes 524288 | tf_op jit(solution)/shard_map/all_to_all | solution.py:12
  39.3 7.1 %collective-permute-start = (bf16[128,4,128]{2,1,0:T(4,128)(2,1)S(1)}, bf16[128,4,128]{2,1,0:T(4,128)(2,1)S(1)}, u32[]{:S(2)}, u32[]{:S(2)}) collective-permute-start(bf16[128,4,128]{2,1,0:T(4,128)(2,1)S(1)} %get-tuple-element.32), channel_id=1, source_target_pairs={{0,1},{1,2},{2,3},{3,4},{4,5},{5,6},{6,7},{7,8},{8,9},{9,10},{10,1... | collective-permute-start | bytes 393224 | tf_op jit(solution)/shard_map/ppermute | solution.py:23
  39.4 7.1 %collective-permute-start.1 = (bf16[128,4,128]{2,1,0:T(4,128)(2,1)S(1)}, bf16[128,4,128]{2,1,0:T(4,128)(2,1)S(1)}, u32[]{:S(2)}, u32[]{:S(2)}) collective-permute-start(bf16[128,4,128]{2,1,0:T(4,128)(2,1)S(1)} %get-tuple-element.33), channel_id=1, source_target_pairs={{1,0},{2,1},{3,2},{4,3},{5,4},{6,5},{7,6},{8,7},{9,8},{10,9},{11,1... | collective-permute-start | bytes 393224 | tf_op jit(solution)/shard_map/ppermute | solution.py:24
